TPU v7x, 512 devices: a whole 4x8x8 slice. The times are simulated.
512 devices in a mesh: gx: 64 (over y, x, z_lo), gy: 8 (over z_hi, core).
Axes of the slice: x: 4, y: 8, z: 8 (z_hi: 4, z_lo: 2; z = z_hi * 2 + z_lo), core: 2. Of those that a mesh axis runs over, the one named last changes fastest.
Arguments:
- droplet_mass: float32 [512, 33, 4, 1024], P('gx', None, None, 'gy'), may hold values from 0.05 to 1
- wind_x: float32 [512, 4, 1024], P('gx', None, 'gy'), may hold values from -0.35 to 0.35
- wind_y: float32 [512, 4, 1024], P('gx', None, 'gy'), may hold values from -0.35 to 0.35
- kernel: float32 [33, 33], replicated, may hold values from 0.01 to 0.08
- breakup: float32 [33, 33], replicated, may hold values from 0.05 to 0.6
- target: int32 [33, 33], replicated, may hold values from 1 to 32, as said below
- fragment_low: int32 [33, 33], replicated, may hold values from 0 to 32, as said below
- cloudy: int32 [512, 8], P('gx', 'gy'), may hold values from 0 to 1, as said below
Outputs:
- mass_out: float32 [512, 33, 4, 1024], P('gx', None, None, 'gy')
Inputs may be any that keep to these rules, and one draw needn't show every extreme that they name: Of the 8 column blocks of one device, at most 4 are cloudy, and some device has exactly 4 cloudy blocks. target[i][j] is min(max(i, j) + 1, 32) or min(max(i, j) + 2, 32). fragment_low[i][j] lies between 0 and min(i, j).
All inputs are finite; a program needn't handle non-finite values.
Results may differ from a plain program's by a relative error of at most 0.00043.
Values sent between devices are 32-bit elements; how exact they have to be, the bound alone decides.
A program may use at most 64 MiB of HBM per device.

v0:
```python
from functools import partial

import jax
import jax.numpy as jnp
from jax import lax
from jax.sharding import PartitionSpec as P

STEPS = 2


def padded_2(shard, sides, width):
    for axis, dim in sides:
        devices, length = (lax.axis_size(axis), shard.shape[dim])
        up = [(i, (i + 1) % devices) for i in range(devices)]
        down = [(j, i) for i, j in up]
        last = lax.slice_in_dim(shard, length - width, length, axis=dim)
        first = lax.slice_in_dim(shard, 0, width, axis=dim)
        before = lax.ppermute(last, axis, up)
        after = lax.ppermute(first, axis, down)
        shard = jnp.concatenate([before, shard, after], axis=dim)
    return shard


def from_behind(shard, axis, by):
    devices = lax.axis_size(axis)
    return lax.ppermute(shard, axis, [(i, (i + by) % devices) for i in range(devices)])


def upwind(courant, behind, behind_two, ahead, ahead_two):
    return jnp.maximum(courant, 0.0) * (1.5 * behind - 0.5 * behind_two) + jnp.minimum(
        courant, 0.0
    ) * (1.5 * ahead - 0.5 * ahead_two)


def tendency(padded, faces_x, faces_y):
    inner_x = padded.shape[0] - 4
    inner_y = padded.shape[3] - 4
    middle_y = padded[:, :, :, 2 : inner_y + 2]
    flux_x = upwind(
        faces_x[:, None],
        middle_y[1 : inner_x + 2],
        middle_y[0 : inner_x + 1],
        middle_y[2 : inner_x + 3],
        middle_y[3 : inner_x + 4],
    )
    middle_x = padded[2 : inner_x + 2]
    flux_y = upwind(
        faces_y[:, None],
        middle_x[..., 1 : inner_y + 2],
        middle_x[..., 0 : inner_y + 1],
        middle_x[..., 2 : inner_y + 3],
        middle_x[..., 3 : inner_y + 4],
    )
    return -(flux_x[1:] - flux_x[:-1]) - (flux_y[..., 1:] - flux_y[..., :-1])


def collision_matrix(kernel, breakup, target, fragment_low):
    count = kernel.shape[0]
    first = lax.broadcasted_iota(jnp.int32, (count, count), 0)
    second = lax.broadcasted_iota(jnp.int32, (count, count), 1)
    larger = jnp.maximum(first, second)
    spread = (larger - fragment_low + 1).astype(jnp.float32)
    levels = jnp.arange(count, dtype=jnp.int32)[:, None, None]
    merged = (levels == target[None]).astype(jnp.float32)
    broken = ((levels >= fragment_low[None]) & (levels <= larger[None])).astype(
        jnp.float32
    ) / spread[None]
    losses = 0.5 * (
        (levels == first[None]).astype(jnp.float32) + (levels == second[None]).astype(jnp.float32)
    )
    portion = (1.0 - breakup)[None] * merged + breakup[None] * broken - losses
    return (kernel[None] * portion).reshape(count, count * count).astype(jnp.bfloat16)


def collide_block(matrix, pieces):
    block, flag = pieces
    cells = block.reshape(block.shape[0], -1)
    products = (
        (cells[:, None, :] * cells[None, :, :])
        .reshape(cells.shape[0] * cells.shape[0], -1)
        .astype(jnp.bfloat16)
    )
    change = jnp.dot(matrix, products, preferred_element_type=jnp.float32).reshape(block.shape)
    return block + flag.astype(jnp.float32) * change


def with_rims(field):
    return padded_2(field, (("gx", 0), ("gy", 3)), 2)


def local(droplet_mass, wind_x, wind_y, kernel, breakup, target, fragment_low, cloudy):
    matrix = collision_matrix(kernel, breakup, target, fragment_low)
    flags = cloudy[:, 0]
    state = droplet_mass
    west = from_behind(wind_x[-1:], "gx", 1)
    south = from_behind(wind_y[:, :, -1:], "gy", 1)
    faces_x = jnp.concatenate([west, wind_x], axis=0)
    faces_y = jnp.concatenate([south, wind_y], axis=2)
    for repeat in range(STEPS):
        first = state + tendency(with_rims(state), faces_x, faces_y)
        state = 0.5 * state + 0.5 * (first + tendency(with_rims(first), faces_x, faces_y))
        state = lax.map(partial(collide_block, matrix), (state, flags))
    return state


def solution(mesh):
    in_specs = (
        P("gx", None, None, "gy"),
        P("gx", None, "gy"),
        P("gx", None, "gy"),
        P(),
        P(),
        P(),
        P(),
        P("gx", "gy"),
    )
    out_specs = P("gx", None, None, "gy")
    return jax.shard_map(local, mesh=mesh, in_specs=in_specs, out_specs=out_specs, check_vma=False)
```

profile of v0, /device:TPU:129, one launch (start us, length us, event | category | flops | bytes accessed | tf_op | source)
XLA Modules:
  0.0 225.9 jit_solution(11030569144983969065)
XLA Ops:
  1.1 4.0 %collective-permute-start.1 = (f32[2,33,4,128]{3,2,1,0:T(4,128)S(1)}, f32[2,33,4,128]{3,2,1,0:T(4,128)S(1)}, u32[]{:S(2)}, u32[]{:S(2)}) collective-permute-start(f32[2,33,4,128]{3,2,1,0:T(4,128)S(1)} %get-tuple-element.238), channel_id=1, source_target_pairs={{0,8},{8,16},{16,24},{24,32},{32,40},{40,48},{48,56},{56,64},{64,7... | collective-permute-start | bytes 405512 | tf_op jit(solution)/shard_map/ppermute | solution.py:18
  5.1 7.0 %collective-permute-start.2 = (f32[2,33,4,128]{3,2,1,0:T(4,128)S(1)}, f32[2,33,4,128]{3,2,1,0:T(4,128)S(1)}, u32[]{:S(2)}, u32[]{:S(2)}) collective-permute-start(f32[2,33,4,128]{3,2,1,0:T(4,128)S(1)} %get-tuple-element.237), channel_id=1, source_target_pairs={{8,0},{16,8},{24,16},{32,24},{40,32},{48,40},{56,48},{64,56},{72,6... | collective-permute-start | bytes 405512 | tf_op jit(solution)/shard_map/ppermute | solution.py:19
  12.9 7.0 %collective-permute-start.3 = (f32[8,4,1]{2,1,0:T(4,128)S(1)}, f32[8,4,1]{2,1,0:T(4,128)S(1)}, u32[]{:S(2)}, u32[]{:S(2)}) collective-permute-start(f32[8,4,1]{2,1,0:T(4,128)S(1)} %slice.259), channel_id=1, source_target_pairs={{0,1},{1,2},{2,3},{3,4},{4,5},{5,6},{6,7},{7,0},{8,9},{9,10},{10,1... | collective-permute-start | bytes 392 | tf_op jit(solution)/shard_map/ppermute | solution.py:26
  33.6 2.2 copy.46
  38.7 5.7 %collective-permute-start.4 = (f32[12,33,4,2]{1,2,3,0:T(4,128)}, f32[12,33,4,2]{1,2,3,0:T(4,128)}, u32[]{:S(2)}, u32[]{:S(2)}) collective-permute-start(f32[12,33,4,2]{1,2,3,0:T(4,128)} %copy.45), channel_id=1, source_target_pairs={{0,1},{1,2},{2,3},{3,4},{4,5},{5,6},{6,7},{7,0},{8,9},{9,10},{10,1... | collective-permute-start | bytes 38024 | tf_op jit(solution)/shard_map/ppermute | solution.py:18
  46.9 2.1 copy.30
  49.0 3.5 %fusion.47 = f32[8,33,4,129]{3,2,1,0:T(4,128)S(1)} fusion(f32[12,33,4,128]{3,2,1,0:T(4,128)S(1)} %get-tuple-element.246, f32[12,33,4,2]{3,2,1,0:T(4,128)S(1)} %copy.32, f32[12,33,4,2]{3,2,1,0:T(4,128)} %copy.30, f32[8,4,129]{2,1,0:T(4,128)S(1)} %copy-done.5, f32[8,4,129]{2,1,0:T(4,128)S(1)} %get-tuple-element.247), kind=kLoop, calls=%fused_computation.77 | loop fusion | flops 1770912 | bytes 1414272 | tf_op jit(solution)/shard_map/add | solution.py:30
  53.0 7.6 %collective-permute-start.7 = (f32[2,33,4,128]{3,2,1,0:T(4,128)S(1)}, f32[2,33,4,128]{3,2,1,0:T(4,128)S(1)}, u32[]{:S(2)}, u32[]{:S(2)}) collective-permute-start(f32[2,33,4,128]{3,2,1,0:T(4,128)S(1)} %get-tuple-element.233), channel_id=1, source_target_pairs={{8,0},{16,8},{24,16},{32,24},{40,32},{48,40},{56,48},{64,56},{72,6... | collective-permute-start | bytes 405512 | tf_op jit(solution)/shard_map/ppermute | solution.py:19
  64.6 6.0 %collective-permute-done.6 = f32[2,33,4,128]{3,2,1,0:T(4,128)S(1)} collective-permute-done((f32[2,33,4,128]{3,2,1,0:T(4,128)S(1)}, f32[2,33,4,128]{3,2,1,0:T(4,128)S(1)}, u32[]{:S(2)}, u32[]{:S(2)}) %collective-permute-start.6) | collective-permute-done | bytes 135200 | tf_op jit(solution)/shard_map/ppermute | solution.py:18
  71.7 6.8 %collective-permute-start.8 = (f32[12,33,4,2]{1,2,3,0:T(4,128)S(1)}, f32[12,33,4,2]{1,2,3,0:T(4,128)S(1)}, u32[]{:S(2)}, u32[]{:S(2)}) collective-permute-start(f32[12,33,4,2]{1,2,3,0:T(4,128)S(1)} %copy.47), channel_id=1, source_target_pairs={{0,1},{1,2},{2,3},{3,4},{4,5},{5,6},{6,7},{7,0},{8,9},{9,10},{10,1... | collective-permute-start | bytes 38024 | tf_op jit(solution)/shard_map/ppermute | solution.py:18
  81.8 4.8 %collective-permute-done.9 = f32[12,33,4,2]{1,2,3,0:T(4,128)} collective-permute-done((f32[12,33,4,2]{1,2,3,0:T(4,128)S(1)}, f32[12,33,4,2]{1,2,3,0:T(4,128)}, u32[]{:S(2)}, u32[]{:S(2)}) %collective-permute-start.9) | collective-permute-done | bytes 12704 | tf_op jit(solution)/shard_map/ppermute | solution.py:19
  87.9 2.7 %maximum_maximum_fusion = (f32[12,33,4,130]{3,2,1,0:T(4,128)S(1)}, f32[12,33,4,130]{3,2,1,0:T(4,128)S(1)}) fusion(f32[2,33,4,128]{3,2,1,0:T(4,128)S(1)} %collective-permute-done.7, f32[8,33,4,128]{3,2,1,0:T(4,128)S(1)} %fusion.112, f32[2,33,4,128]{3,2,1,0:T(4,128)} %copy-done.2, f32[12,33,4,2]{3,2,1,0:T(4,128)S(1)} %copy.34, f32[12,33,4,2]{3,2,1,0:T(4,128)S(1)} %copy.36), kind=kLoop, calls=%fused_computation.56 | loop fusion | flops 1235520 | bytes 2483712 | tf_op jit(solution)/shard_map/concatenate | solution.py:20
  92.3 30.7 %while.22 = (s32[]{:T(128)}, f32[8,33,4,128]{3,2,1,0:T(4,128)S(1)}, f32[8,33,4,128]{3,2,1,0:T(4,128)S(1)}, s32[8]{0:T(128)}, s32[1089]{0:T(1024)}, /*index=5*/f3...) while((s32[]{:T(128)}, f32[8,33,4,128]{3,2,1,0:T(4,128)S(1)}, ...), condition=%wide.region_1.2_spmd.clone, body=%wide.region_0.1_spmd.clone.sunk | while | flops 38595280 | bytes 5421533 | solution.py:102
  125.0 7.8 %collective-permute-start.11 = (f32[2,33,4,128]{3,2,1,0:T(4,128)S(1)}, f32[2,33,4,128]{3,2,1,0:T(4,128)S(1)}, u32[]{:S(2)}, u32[]{:S(2)}) collective-permute-start(f32[2,33,4,128]{3,2,1,0:T(4,128)S(1)} %get-tuple-element.230), channel_id=1, source_target_pairs={{8,0},{16,8},{24,16},{32,24},{40,32},{48,40},{56,48},{64,56},{72,6... | collective-permute-start | bytes 405512 | tf_op jit(solution)/shard_map/ppermute | solution.py:19
  136.0 2.2 copy.50
  141.2 5.7 %collective-permute-start.12 = (f32[12,33,4,2]{1,2,3,0:T(4,128)}, f32[12,33,4,2]{1,2,3,0:T(4,128)}, u32[]{:S(2)}, u32[]{:S(2)}) collective-permute-start(f32[12,33,4,2]{1,2,3,0:T(4,128)} %copy.49), channel_id=1, source_target_pairs={{0,1},{1,2},{2,3},{3,4},{4,5},{5,6},{6,7},{7,0},{8,9},{9,10},{10,1... | collective-permute-start | bytes 38024 | tf_op jit(solution)/shard_map/ppermute | solution.py:18
  148.6 2.1 copy.38
  150.8 3.5 %fusion.38 = f32[8,33,4,129]{3,2,1,0:T(4,128)S(1)} fusion(f32[12,33,4,128]{3,2,1,0:T(4,128)S(1)} %get-tuple-element.242, f32[12,33,4,2]{3,2,1,0:T(4,128)S(1)} %copy.40, f32[12,33,4,2]{3,2,1,0:T(4,128)} %copy.38, f32[8,4,129]{2,1,0:T(4,128)S(1)} %copy-done.6, f32[8,4,129]{2,1,0:T(4,128)S(1)} %copy-done.4), kind=kLoop, calls=%fused_computation.68 | loop fusion | flops 1770912 | bytes 1414272 | tf_op jit(solution)/shard_map/add | solution.py:30
  154.7 8.2 %collective-permute-start.15 = (f32[2,33,4,128]{3,2,1,0:T(4,128)S(1)}, f32[2,33,4,128]{3,2,1,0:T(4,128)S(1)}, u32[]{:S(2)}, u32[]{:S(2)}) collective-permute-start(f32[2,33,4,128]{3,2,1,0:T(4,128)S(1)} %get-tuple-element.226), channel_id=1, source_target_pairs={{8,0},{16,8},{24,16},{32,24},{40,32},{48,40},{56,48},{64,56},{72,6... | collective-permute-start | bytes 405512 | tf_op jit(solution)/shard_map/ppermute | solution.py:19
  164.9 8.1 %collective-permute-done.14 = f32[2,33,4,128]{3,2,1,0:T(4,128)S(1)} collective-permute-done((f32[2,33,4,128]{3,2,1,0:T(4,128)S(1)}, f32[2,33,4,128]{3,2,1,0:T(4,128)S(1)}, u32[]{:S(2)}, u32[]{:S(2)}) %collective-permute-start.14) | collective-permute-done | bytes 135200 | tf_op jit(solution)/shard_map/ppermute | solution.py:18
  174.1 7.5 %collective-permute-start.16 = (f32[12,33,4,2]{1,2,3,0:T(4,128)S(1)}, f32[12,33,4,2]{1,2,3,0:T(4,128)S(1)}, u32[]{:S(2)}, u32[]{:S(2)}) collective-permute-start(f32[12,33,4,2]{1,2,3,0:T(4,128)S(1)} %copy.51), channel_id=1, source_target_pairs={{0,1},{1,2},{2,3},{3,4},{4,5},{5,6},{6,7},{7,0},{8,9},{9,10},{10,1... | collective-permute-start | bytes 38024 | tf_op jit(solution)/shard_map/ppermute | solution.py:18
  185.6 3.9 %collective-permute-done.17 = f32[12,33,4,2]{1,2,3,0:T(4,128)S(1)} collective-permute-done((f32[12,33,4,2]{1,2,3,0:T(4,128)S(1)}, f32[12,33,4,2]{1,2,3,0:T(4,128)S(1)}, u32[]{:S(2)}, u32[]{:S(2)}) %collective-permute-start.17) | collective-permute-done | bytes 12704 | tf_op jit(solution)/shard_map/ppermute | solution.py:19
  190.0 2.6 %maximum_maximum_fusion.1 = (f32[12,33,4,130]{3,2,1,0:T(4,128)S(1)}, f32[12,33,4,130]{3,2,1,0:T(4,128)S(1)}) fusion(f32[2,33,4,128]{3,2,1,0:T(4,128)S(1)} %collective-permute-done.15, f32[8,33,4,128]{3,2,1,0:T(4,128)S(1)} %fusion.104, f32[2,33,4,128]{3,2,1,0:T(4,128)S(1)} %collective-permute-done.14, f32[12,33,4,2]{3,2,1,0:T(4,128)S(1)} %copy.42, ...), kind=kLoop, calls=%fused_computation.62 | loop fusion | flops 1235520 | bytes 2483712 | tf_op jit(solution)/shard_map/concatenate | solution.py:20
  194.4 30.7 %while.23 = (s32[]{:T(128)}, f32[8,33,4,128]{3,2,1,0:T(4,128)S(1)}, f32[8,33,4,128]{3,2,1,0:T(4,128)S(1)}, s32[8]{0:T(128)}, s32[1089]{0:T(1024)}, /*index=5*/f3...) while((s32[]{:T(128)}, f32[8,33,4,128]{3,2,1,0:T(4,128)S(1)}, ...), condition=%wide.region_3.4_spmd.clone, body=%wide.region_2.3_spmd.clone.sunk | while | flops 38595280 | bytes 5421533 | solution.py:102
  (257 shorter events, 102.5 us)
Async XLA Ops:
  0.0 31.8 %copy-start = (f32[8,33,4,128]{3,2,1,0:T(4,128)S(1)}, f32[8,33,4,128]{3,2,1,0:T(4,128)}, u32[]{:S(2)}) copy-start(f32[8,33,4,128]{3,2,1,0:T(4,128)} %param.12) | copy-start | bytes 1622020
  1.1 30.7 %collective-permute-start.1 = (f32[2,33,4,128]{3,2,1,0:T(4,128)S(1)}, f32[2,33,4,128]{3,2,1,0:T(4,128)S(1)}, u32[]{:S(2)}, u32[]{:S(2)}) collective-permute-start(f32[2,33,4,128]{3,2,1,0:T(4,128)S(1)} %get-tuple-element.238), channel_id=1, source_target_pairs={{0,8},{8,16},{16,24},{24,32},{32,40},{40,48},{48,56},{56,64},{64,7... | collective-permute-start | bytes 405512 | tf_op jit(solution)/shard_map/ppermute | solution.py:18
  5.1 27.1 %collective-permute-start.2 = (f32[2,33,4,128]{3,2,1,0:T(4,128)S(1)}, f32[2,33,4,128]{3,2,1,0:T(4,128)S(1)}, u32[]{:S(2)}, u32[]{:S(2)}) collective-permute-start(f32[2,33,4,128]{3,2,1,0:T(4,128)S(1)} %get-tuple-element.237), channel_id=1, source_target_pairs={{8,0},{16,8},{24,16},{32,24},{40,32},{48,40},{56,48},{64,56},{72,6... | collective-permute-start | bytes 405512 | tf_op jit(solution)/shard_map/ppermute | solution.py:19
  12.9 16.1 %collective-permute-start.3 = (f32[8,4,1]{2,1,0:T(4,128)S(1)}, f32[8,4,1]{2,1,0:T(4,128)S(1)}, u32[]{:S(2)}, u32[]{:S(2)}) collective-permute-start(f32[8,4,1]{2,1,0:T(4,128)S(1)} %slice.259), channel_id=1, source_target_pairs={{0,1},{1,2},{2,3},{3,4},{4,5},{5,6},{6,7},{7,0},{8,9},{9,10},{10,1... | collective-permute-start | bytes 392 | tf_op jit(solution)/shard_map/ppermute | solution.py:26
  20.5 9.9 %collective-permute-start = (f32[1,4,128]{2,1,0:T(4,128)S(1)}, f32[1,4,128]{2,1,0:T(4,128)S(1)}, u32[]{:S(2)}, u32[]{:S(2)}) collective-permute-start(f32[1,4,128]{2,1,0:T(4,128)S(1)} %slice.250), channel_id=1, source_target_pairs={{0,8},{8,16},{16,24},{24,32},{32,40},{40,48},{48,56},{56,64},{64,7... | collective-permute-start | bytes 6152 | tf_op jit(solution)/shard_map/ppermute | solution.py:26
  28.3 35.7 %copy-start.13 = (s32[1089]{0:T(1024)}, s32[1089]{0:T(1024)S(1)}, u32[]{:S(2)}) copy-start(s32[1089]{0:T(1024)S(1)} %iota.45) | copy-start | bytes 13072
  30.4 60.2 %copy-start.3 = (f32[8,4,129]{2,1,0:T(4,128)}, f32[8,4,129]{2,1,0:T(4,128)S(1)}, u32[]{:S(2)}) copy-start(f32[8,4,129]{2,1,0:T(4,128)S(1)} %get-tuple-element.247) | copy-start | bytes 49540
  35.7 9.8 %collective-permute-start.5 = (f32[12,33,4,2]{1,2,3,0:T(4,128)}, f32[12,33,4,2]{1,2,3,0:T(4,128)}, u32[]{:S(2)}, u32[]{:S(2)}) collective-permute-start(f32[12,33,4,2]{1,2,3,0:T(4,128)} %copy.46), channel_id=1, source_target_pairs={{1,0},{2,1},{3,2},{4,3},{5,4},{6,5},{7,6},{0,7},{9,8},{10,9},{11,1... | collective-permute-start | bytes 38024 | tf_op jit(solution)/shard_map/ppermute | solution.py:19
  38.7 8.1 %collective-permute-start.4 = (f32[12,33,4,2]{1,2,3,0:T(4,128)}, f32[12,33,4,2]{1,2,3,0:T(4,128)}, u32[]{:S(2)}, u32[]{:S(2)}) collective-permute-start(f32[12,33,4,2]{1,2,3,0:T(4,128)} %copy.45), channel_id=1, source_target_pairs={{0,1},{1,2},{2,3},{3,4},{4,5},{5,6},{6,7},{7,0},{8,9},{9,10},{10,1... | collective-permute-start | bytes 38024 | tf_op jit(solution)/shard_map/ppermute | solution.py:18
  52.6 11.4 %copy-start.14 = (s32[1089]{0:T(1024)S(1)}, s32[1089]{0:T(1024)}, u32[]{:S(2)}) copy-start(s32[1089]{0:T(1024)} %iota.47) | copy-start | bytes 13072
  53.0 11.5 %collective-permute-start.7 = (f32[2,33,4,128]{3,2,1,0:T(4,128)S(1)}, f32[2,33,4,128]{3,2,1,0:T(4,128)S(1)}, u32[]{:S(2)}, u32[]{:S(2)}) collective-permute-start(f32[2,33,4,128]{3,2,1,0:T(4,128)S(1)} %get-tuple-element.233), channel_id=1, source_target_pairs={{8,0},{16,8},{24,16},{32,24},{40,32},{48,40},{56,48},{64,56},{72,6... | collective-permute-start | bytes 405512 | tf_op jit(solution)/shard_map/ppermute | solution.py:19
  60.6 10.0 %collective-permute-start.6 = (f32[2,33,4,128]{3,2,1,0:T(4,128)S(1)}, f32[2,33,4,128]{3,2,1,0:T(4,128)S(1)}, u32[]{:S(2)}, u32[]{:S(2)}) collective-permute-start(f32[2,33,4,128]{3,2,1,0:T(4,128)S(1)} %get-tuple-element.232), channel_id=1, source_target_pairs={{0,8},{8,16},{16,24},{24,32},{32,40},{40,48},{48,56},{56,64},{64,7... | collective-permute-start | bytes 405512 | tf_op jit(solution)/shard_map/ppermute | solution.py:18
  71.7 9.6 %collective-permute-start.8 = (f32[12,33,4,2]{1,2,3,0:T(4,128)S(1)}, f32[12,33,4,2]{1,2,3,0:T(4,128)S(1)}, u32[]{:S(2)}, u32[]{:S(2)}) collective-permute-start(f32[12,33,4,2]{1,2,3,0:T(4,128)S(1)} %copy.47), channel_id=1, source_target_pairs={{0,1},{1,2},{2,3},{3,4},{4,5},{5,6},{6,7},{7,0},{8,9},{9,10},{10,1... | collective-permute-start | bytes 38024 | tf_op jit(solution)/shard_map/ppermute | solution.py:18
  79.0 7.6 %collective-permute-start.9 = (f32[12,33,4,2]{1,2,3,0:T(4,128)S(1)}, f32[12,33,4,2]{1,2,3,0:T(4,128)}, u32[]{:S(2)}, u32[]{:S(2)}) collective-permute-start(f32[12,33,4,2]{1,2,3,0:T(4,128)S(1)} %copy.48), channel_id=1, source_target_pairs={{1,0},{2,1},{3,2},{4,3},{5,4},{6,5},{7,6},{0,7},{9,8},{10,9},{11,1... | collective-permute-start | bytes 38024 | tf_op jit(solution)/shard_map/ppermute | solution.py:19
  123.1 10.0 %collective-permute-start.10 = (f32[2,33,4,128]{3,2,1,0:T(4,128)S(1)}, f32[2,33,4,128]{3,2,1,0:T(4,128)S(1)}, u32[]{:S(2)}, u32[]{:S(2)}) collective-permute-start(f32[2,33,4,128]{3,2,1,0:T(4,128)S(1)} %get-tuple-element.231), channel_id=1, source_target_pairs={{0,8},{8,16},{16,24},{24,32},{32,40},{40,48},{48,56},{56,64},{64,7... | collective-permute-start | bytes 405512 | tf_op jit(solution)/shard_map/ppermute | solution.py:18
  125.0 9.6 %collective-permute-start.11 = (f32[2,33,4,128]{3,2,1,0:T(4,128)S(1)}, f32[2,33,4,128]{3,2,1,0:T(4,128)S(1)}, u32[]{:S(2)}, u32[]{:S(2)}) collective-permute-start(f32[2,33,4,128]{3,2,1,0:T(4,128)S(1)} %get-tuple-element.230), channel_id=1, source_target_pairs={{8,0},{16,8},{24,16},{32,24},{40,32},{48,40},{56,48},{64,56},{72,6... | collective-permute-start | bytes 405512 | tf_op jit(solution)/shard_map/ppermute | solution.py:19
  136.0 10.9 %copy-start.9 = (f32[9,4,128]{2,1,0:T(4,128)S(1)}, f32[9,4,128]{2,1,0:T(4,128)}, u32[]{:S(2)}) copy-start(f32[9,4,128]{2,1,0:T(4,128)} %get-tuple-element.249) | copy-start | bytes 55300
  136.0 10.9 %copy-start.11 = (f32[9,4,128]{2,1,0:T(4,128)S(1)}, f32[9,4,128]{2,1,0:T(4,128)}, u32[]{:S(2)}) copy-start(f32[9,4,128]{2,1,0:T(4,128)} %get-tuple-element.250) | copy-start | bytes 55300
  138.2 9.1 %collective-permute-start.13 = (f32[12,33,4,2]{1,2,3,0:T(4,128)}, f32[12,33,4,2]{1,2,3,0:T(4,128)}, u32[]{:S(2)}, u32[]{:S(2)}) collective-permute-start(f32[12,33,4,2]{1,2,3,0:T(4,128)} %copy.50), channel_id=1, source_target_pairs={{1,0},{2,1},{3,2},{4,3},{5,4},{6,5},{7,6},{0,7},{9,8},{10,9},{11,1... | collective-permute-start | bytes 38024 | tf_op jit(solution)/shard_map/ppermute | solution.py:19
  141.2 7.4 %collective-permute-start.12 = (f32[12,33,4,2]{1,2,3,0:T(4,128)}, f32[12,33,4,2]{1,2,3,0:T(4,128)}, u32[]{:S(2)}, u32[]{:S(2)}) collective-permute-start(f32[12,33,4,2]{1,2,3,0:T(4,128)} %copy.49), channel_id=1, source_target_pairs={{0,1},{1,2},{2,3},{3,4},{4,5},{5,6},{6,7},{7,0},{8,9},{9,10},{10,1... | collective-permute-start | bytes 38024 | tf_op jit(solution)/shard_map/ppermute | solution.py:18
  154.7 10.2 %collective-permute-start.15 = (f32[2,33,4,128]{3,2,1,0:T(4,128)S(1)}, f32[2,33,4,128]{3,2,1,0:T(4,128)S(1)}, u32[]{:S(2)}, u32[]{:S(2)}) collective-permute-start(f32[2,33,4,128]{3,2,1,0:T(4,128)S(1)} %get-tuple-element.226), channel_id=1, source_target_pairs={{8,0},{16,8},{24,16},{32,24},{40,32},{48,40},{56,48},{64,56},{72,6... | collective-permute-start | bytes 405512 | tf_op jit(solution)/shard_map/ppermute | solution.py:19
  163.0 10.1 %collective-permute-start.14 = (f32[2,33,4,128]{3,2,1,0:T(4,128)S(1)}, f32[2,33,4,128]{3,2,1,0:T(4,128)S(1)}, u32[]{:S(2)}, u32[]{:S(2)}) collective-permute-start(f32[2,33,4,128]{3,2,1,0:T(4,128)S(1)} %get-tuple-element.225), channel_id=1, source_target_pairs={{0,8},{8,16},{16,24},{24,32},{32,40},{40,48},{48,56},{56,64},{64,7... | collective-permute-start | bytes 405512 | tf_op jit(solution)/shard_map/ppermute | solution.py:18
  174.1 11.0 %collective-permute-start.16 = (f32[12,33,4,2]{1,2,3,0:T(4,128)S(1)}, f32[12,33,4,2]{1,2,3,0:T(4,128)S(1)}, u32[]{:S(2)}, u32[]{:S(2)}) collective-permute-start(f32[12,33,4,2]{1,2,3,0:T(4,128)S(1)} %copy.51), channel_id=1, source_target_pairs={{0,1},{1,2},{2,3},{3,4},{4,5},{5,6},{6,7},{7,0},{8,9},{9,10},{10,1... | collective-permute-start | bytes 38024 | tf_op jit(solution)/shard_map/ppermute | solution.py:18
  182.0 7.5 %collective-permute-start.17 = (f32[12,33,4,2]{1,2,3,0:T(4,128)S(1)}, f32[12,33,4,2]{1,2,3,0:T(4,128)S(1)}, u32[]{:S(2)}, u32[]{:S(2)}) collective-permute-start(f32[12,33,4,2]{1,2,3,0:T(4,128)S(1)} %copy.52), channel_id=1, source_target_pairs={{1,0},{2,1},{3,2},{4,3},{5,4},{6,5},{7,6},{0,7},{9,8},{10,9},{11,1... | collective-permute-start | bytes 38024 | tf_op jit(solution)/shard_map/ppermute | solution.py:19
  (10 other events, 62.7 us)
where the time goes:
time: 229 us; the launch traced here: 226 us
  starting transfers between devices  82.7 us (36%)
  local copies, waits for them, and re-layouts  60.2 us (26%)
  other arithmetic  28.4 us (12%)
  waiting for transfers between devices  24.4 us (11%)
  matrix products  18.1 us (8%)
  loops' own time  11.6 us (5%)
    ppermute x8, starting transfers between devices, padded_2(): after = lax.ppermute(first, axis, down)  38.3 us
    ppermute x8, starting transfers between devices, padded_2(): before = lax.ppermute(last, axis, up)  35.6 us
    dynamic_slice x16, local copies, waits for them, and re-layouts, local(): state = lax.map(partial(collide_block, matrix), (state, flags))  19.9 us
    dot_general x16, matrix products, collide_block(): jnp.dot(matrix, products, preferred_element_type=jnp.float32)  18.1 us
    ppermute x8, waiting for transfers between devices, padded_2(): before = lax.ppermute(last, axis, up)  14.4 us
    add x8, other arithmetic, upwind(): jnp.maximum(courant, 0.0) * (1.5 * behind - 0.5 * behind_two)  12.5 us
    another operation x2, loops' own time, local(): state = lax.map(partial(collide_block, matrix), (state, flags))  11.6 us
    ppermute x8, waiting for transfers between devices, padded_2(): after = lax.ppermute(first, axis, down)  9.99 us
  transfers between devices with their start and end apart: 18, of which 6 were waited for; matrix products, arithmetic and copies ran while one was open for 10% of the time, Pallas kernels for 0%

commit v1 on v0

v1 whole, which is shorter than its diff:
```python
import functools

import jax
import jax.numpy as jnp
from jax import lax
from jax.experimental import pallas as pl
from jax.experimental.pallas import tpu as pltpu
from jax.sharding import PartitionSpec as P

STEPS = 2
STAGES = 2 * STEPS
BINS = 33
MAIN = 32
LEVELS = 4
CX = 8
CY = 128
CAP = 4
DEPTH = 688
ROWS = 48
EDGE = 2 * MAIN + CX
MESH = pl.DeviceIdType.MESH


def pair_pieces():
    pieces = []
    for a in range(8):
        pieces.append((32 * a, a, 0, 32))
        pieces.append((32 * (8 + a), 24 + a, 24, 32))
        pieces.append((32 * (8 + a) + 8, 8 + a, 8, 32))
    for a in range(4):
        pieces.append((32 * (16 + a), 20 + a, 16, 32))
        pieces.append((32 * (16 + a) + 16, 16 + a, 16, 32))
    pieces.append((32 * 20, 32, 0, 32))
    pieces.append((32 * 21, 32, 32, 33))
    return pieces


def build_matrix(tables, padded, flipped, parts, matrix):
    for n, table in enumerate(tables):
        padded[n] = jnp.zeros((128, 128), jnp.float32)
        padded[n, 0:BINS, 0:BINS] = table[...].astype(jnp.float32)
        flipped[n] = padded[n].T
    out_bin = lax.broadcasted_iota(jnp.int32, (ROWS, 128), 0).astype(jnp.float32)
    second = lax.broadcasted_iota(jnp.int32, (ROWS, 128), 1)
    lanes = lax.broadcasted_iota(jnp.int32, (1, 128), 1)

    def one(i, carry):
        first = jnp.full((1, 128), i, jnp.int32).astype(jnp.float32)
        larger = jnp.maximum(first, lanes.astype(jnp.float32))
        losses = 0.5 * jnp.where(out_bin == first, 1.0, 0.0) + 0.5 * jnp.where(
            out_bin == second.astype(jnp.float32), 1.0, 0.0
        )

        def rates(source):
            kern, brk, tgt, low = (source[n, pl.ds(i, 1), :] for n in range(4))
            each = brk * (1.0 / (larger - low + 1.0))
            merged = jnp.where(out_bin == tgt, 1.0 - brk, 0.0)
            broken = jnp.where((out_bin >= low) & (out_bin <= larger), each, 0.0)
            rounded = (kern * (merged + broken - losses)).astype(jnp.bfloat16)
            return rounded.astype(jnp.float32)

        start = jnp.where(i == MAIN, 0, (i // 8) * 8 + 8)
        end = jnp.where(i == MAIN, MAIN, BINS)
        both = (second >= start) & (second < end)
        parts[i] = rates(padded) + jnp.where(both, rates(flipped), 0.0)
        return carry

    lax.fori_loop(0, BINS, one, 0)
    for tile in range(0, DEPTH, 128):
        acc = jnp.zeros((ROWS, 128), jnp.float32)
        for place, i, low, high in pair_pieces():
            at = place - tile
            if 0 <= at < 128:
                moved = pltpu.roll(parts[i], (at - low) % 128, 1)
                acc = jnp.where((second >= at) & (second < at + high - low), moved, acc)
        width = min(128, DEPTH - tile)
        high = acc.astype(jnp.bfloat16)
        rest = (acc - high.astype(jnp.float32)).astype(jnp.bfloat16)
        matrix[0:ROWS, tile : tile + width] = high[:, :width]
        matrix[ROWS : 2 * ROWS, tile : tile + width] = rest[:, :width]


def kernel(
    size_x,
    size_y,
    mass,
    wind_x,
    wind_y,
    table_kernel,
    table_breakup,
    table_target,
    table_low,
    cloudy,
    out,
    state,
    last,
    moved,
    moved_last,
    coef,
    send_x,
    send_y,
    got_x,
    got_y,
    got_wx,
    got_wy,
    padded,
    flipped,
    parts,
    matrix,
    products,
    change,
    sem_sx,
    sem_rx,
    sem_sy,
    sem_ry,
    sem_sw,
    sem_rw,
):
    gx = lax.axis_index("gx")
    gy = lax.axis_index("gy")
    west = (lax.rem(gx + size_x - 1, size_x), gy)
    east = (lax.rem(gx + 1, size_x), gy)
    south = (gx, lax.rem(gy + size_y - 1, size_y))
    north = (gx, lax.rem(gy + 1, size_y))
    lane = lax.broadcasted_iota(jnp.int32, (CX, CY), 1)
    row = lax.broadcasted_iota(jnp.int32, (CX, CY), 0)
    wide = lax.broadcasted_iota(jnp.int32, (MAIN, CY), 1)

    def remote(src, dst, send, recv, device):
        return pltpu.make_async_remote_copy(
            src_ref=src, dst_ref=dst, send_sem=send, recv_sem=recv, device_id=device, device_id_type=MESH
        )

    def copies(stage, level):
        out = []
        for side, device in ((0, west), (1, east)):
            out.append(
                remote(
                    send_x.at[stage, level, side],
                    got_x.at[stage, level, 1 - side],
                    sem_sx.at[stage, level, side],
                    sem_rx.at[stage, level, 1 - side],
                    device,
                )
            )
        for side, device in ((0, south), (1, north)):
            out.append(
                remote(
                    send_y.at[stage, level],
                    got_y.at[stage, level, 1 - side],
                    sem_sy.at[stage, level, side],
                    sem_ry.at[stage, level, 1 - side],
                    device,
                )
            )
        return out

    def wind_copies():
        return [
            remote(wind_x.at[pl.ds(24, 8)], got_wx, sem_sw.at[0], sem_rw.at[0], east),
            remote(wind_y, got_wy, sem_sw.at[1], sem_rw.at[1], north),
        ]

    def keep(stage, level, values, tail):
        pack = jnp.zeros((CX, CY), jnp.float32)
        for x in range(CX):
            value = values(x)
            state[stage, level, x] = value
            if x < 2:
                send_x[stage, level, 0, x * MAIN : (x + 1) * MAIN] = value
            if x >= CX - 2:
                at = x - (CX - 2)
                send_x[stage, level, 1, at * MAIN : (at + 1) * MAIN] = value
            for j in range(4):
                at = 32 * j + 4 * x
                turned = pltpu.roll(value[8 * j : 8 * j + 8], (at - 126) % 128, 1)
                pack = jnp.where((lane >= at) & (lane < at + 4), turned, pack)
        send_x[stage, level, 0, 2 * MAIN : EDGE] = tail
        send_x[stage, level, 1, 2 * MAIN : EDGE] = tail
        send_y[stage, level, 0:CX] = pack
        send_y[stage, level, CX : 2 * CX] = tail

    barrier = pltpu.get_barrier_semaphore()
    for device in (west, east, south, north):
        pl.semaphore_signal(barrier, inc=1, device_id=device, device_id_type=MESH)

    def load(level, carry):
        tail = mass[pl.ds(4 * MAIN + level, CX, stride=4 * BINS), :]
        last[0, level] = tail
        keep(0, level, lambda x: mass[pl.ds(x * 4 * BINS + level, MAIN, stride=4), :], tail)
        return carry

    lax.fori_loop(0, LEVELS, load, 0)
    pl.semaphore_wait(barrier, 4)
    for copy in wind_copies():
        copy.start()

    def send_first(level, carry):
        for copy in copies(0, level):
            copy.start()
        return carry

    lax.fori_loop(0, LEVELS, send_first, 0)

    build_matrix((table_kernel, table_breakup, table_target, table_low), padded, flipped, parts, matrix)

    flags = [cloudy[x, 0] for x in range(CX)]
    count = jnp.int32(0)
    chosen = [jnp.int32(0)] * CAP
    slots = []
    for x in range(CX):
        slots.append(jnp.minimum(count, CAP - 1))
        for r in range(CAP):
            chosen[r] = jnp.where((flags[x] > 0) & (count == r), x, chosen[r])
        count = count + flags[x]
    live = [flags[x].astype(jnp.float32) for x in range(CX)]

    for copy in wind_copies():
        copy.wait_recv()

    def coefficients(level, carry):
        right = wind_x[pl.ds(level, CX, stride=LEVELS), :]
        left = jnp.where(row == 0, got_wx[pl.ds(4 + level, 1), :], pltpu.roll(right, 1, 0))
        above = wind_y[pl.ds(level, CX, stride=LEVELS), :]
        ghost = got_wy[pl.ds(level, CX, stride=LEVELS), :]
        below = pltpu.roll(jnp.where(lane == CY - 1, ghost, above), 1, 1)

        def five(low, high):
            plus_low, minus_low = jnp.maximum(low, 0.0), jnp.minimum(low, 0.0)
            plus_high, minus_high = jnp.maximum(high, 0.0), jnp.minimum(high, 0.0)
            return (
                -0.5 * plus_low,
                1.5 * plus_low + 0.5 * plus_high,
                1.5 * minus_low - 1.5 * plus_high,
                -0.5 * minus_low - 1.5 * minus_high,
                0.5 * minus_high,
            )

        in_x = five(left, right)
        in_y = five(below, above)
        for n, value in enumerate(
            (in_x[0], in_x[1], in_x[3], in_x[4], in_y[0], in_y[1], in_y[3], in_y[4], 1.0 + (in_x[2] + in_y[2]))
        ):
            coef[level, n] = value
        return carry

    lax.fori_loop(0, LEVELS, coefficients, 0)

    def advance(stage, level):
        edge = jnp.where(lax.rem(lane, 4) < 2, got_y[stage, level, 0, 0:CX], got_y[stage, level, 1, 0:CX])

        def at_x(x):
            if x < 0:
                return got_x[stage, level, 0, (x + 2) * MAIN : (x + 3) * MAIN]
            if x >= CX:
                return got_x[stage, level, 1, (x - CX) * MAIN : (x - CX + 1) * MAIN]
            return state[stage, level, x]

        def value(x):
            c = [coef[level, n, x : x + 1, :] for n in range(9)]
            q = at_x(x)
            acc = c[8] * q
            acc += c[0] * at_x(x - 2) + c[1] * at_x(x - 1)
            acc += c[2] * at_x(x + 1) + c[3] * at_x(x + 2)
            ends = jnp.concatenate(
                [pltpu.roll(edge, (126 - 32 * j - 4 * x) % 128, 1) for j in range(4)], axis=0
            )
            acc += c[4] * pltpu.roll(jnp.where(wide >= CY - 2, ends, q), 2, 1)
            acc += c[5] * pltpu.roll(jnp.where(wide >= CY - 1, ends, q), 1, 1)
            acc += c[6] * pltpu.roll(jnp.where(wide < 1, ends, q), CY - 1, 1)
            acc += c[7] * pltpu.roll(jnp.where(wide < 2, ends, q), CY - 2, 1)
            return acc

        c = [coef[level, n] for n in range(9)]
        e = last[stage, level]
        below_x = got_x[stage, level, 0, 2 * MAIN : EDGE]
        above_x = got_x[stage, level, 1, 2 * MAIN : EDGE]
        below_y = got_y[stage, level, 0, CX : 2 * CX]
        above_y = got_y[stage, level, 1, CX : 2 * CX]
        acc = c[8] * e
        acc += c[0] * pltpu.roll(jnp.where(row >= CX - 2, below_x, e), 2, 0)
        acc += c[1] * pltpu.roll(jnp.where(row >= CX - 1, below_x, e), 1, 0)
        acc += c[2] * pltpu.roll(jnp.where(row < 1, above_x, e), CX - 1, 0)
        acc += c[3] * pltpu.roll(jnp.where(row < 2, above_x, e), CX - 2, 0)
        acc += c[4] * pltpu.roll(jnp.where(lane >= CY - 2, below_y, e), 2, 1)
        acc += c[5] * pltpu.roll(jnp.where(lane >= CY - 1, below_y, e), 1, 1)
        acc += c[6] * pltpu.roll(jnp.where(lane < 1, above_y, e), CY - 1, 1)
        acc += c[7] * pltpu.roll(jnp.where(lane < 2, above_y, e), CY - 2, 1)
        return value, acc

    def collide():
        for r in range(CAP):
            x = chosen[r]
            cols = slice(r * CY, (r + 1) * CY)
            n = moved[x]
            e = moved_last[pl.ds(x, 1), :]

            def bin_of(i):
                return moved[x, i : i + 1, :]

            for a in range(8):
                products[32 * a : 32 * a + 32, cols] = (bin_of(a) * n).astype(jnp.bfloat16)
                products[32 * (8 + a) : 32 * (9 + a), cols] = jnp.concatenate(
                    [bin_of(24 + a) * n[24:32], bin_of(8 + a) * n[8:32]], axis=0
                ).astype(jnp.bfloat16)
            for a in range(4):
                products[32 * (16 + a) : 32 * (17 + a), cols] = jnp.concatenate(
                    [bin_of(20 + a) * n[16:32], bin_of(16 + a) * n[16:32]], axis=0
                ).astype(jnp.bfloat16)
            products[640:672, cols] = (e * n).astype(jnp.bfloat16)
            products[672:688, cols] = jnp.broadcast_to(e * e, (16, CY)).astype(jnp.bfloat16)
        result = jnp.dot(matrix[...], products[...], preferred_element_type=jnp.float32)
        for r in range(CAP):
            cols = slice(r * CY, (r + 1) * CY)
            change[r] = result[0:ROWS, cols] + result[ROWS : 2 * ROWS, cols]

    for stage in range(STAGES):

        def step(level, carry, stage=stage):
            for copy in copies(stage, level):
                copy.wait_recv()
            value, tail = advance(stage, level)
            if stage % 2 == 0:
                last[stage + 1, level] = tail
                keep(stage + 1, level, value, tail)
            else:
                for x in range(CX):
                    moved[x] = 0.5 * state[stage - 1, level, x] + 0.5 * value(x)
                moved_last[...] = 0.5 * last[stage - 1, level] + 0.5 * tail
                collide()

                def after(x):
                    return moved[x] + live[x] * change[slots[x], 0:MAIN]

                for x in range(CX):
                    moved_last[x : x + 1, :] = (
                        moved_last[x : x + 1, :] + live[x] * change[slots[x], MAIN : MAIN + 1]
                    )
                tail = moved_last[...]
                if stage < STAGES - 1:
                    last[stage + 1, level] = tail
                    keep(stage + 1, level, after, tail)
                else:
                    for x in range(CX):
                        out[pl.ds(x * 4 * BINS + level, MAIN, stride=4), :] = after(x)
                    out[pl.ds(4 * MAIN + level, CX, stride=4 * BINS), :] = tail
            if stage < STAGES - 1:
                for copy in copies(stage + 1, level):
                    copy.start()
            return carry

        lax.fori_loop(0, LEVELS, step, 0)

    for copy in wind_copies():
        copy.wait_send()
    for stage in range(STAGES):

        def finish(level, carry, stage=stage):
            for copy in copies(stage, level):
                copy.wait_send()
            return carry

        lax.fori_loop(0, LEVELS, finish, 0)


def local(size_x, size_y, droplet_mass, wind_x, wind_y, table, breakup, target, fragment_low, cloudy):
    vmem = pl.BlockSpec(memory_space=pltpu.VMEM)
    f32 = jnp.float32
    result = pl.pallas_call(
        functools.partial(kernel, size_x, size_y),
        out_shape=jax.ShapeDtypeStruct((CX * BINS * LEVELS, CY), f32),
        in_specs=[vmem] * 7 + [pl.BlockSpec(memory_space=pltpu.SMEM)],
        out_specs=vmem,
        scratch_shapes=[
            pltpu.VMEM((STAGES, LEVELS, CX, MAIN, CY), f32),
            pltpu.VMEM((STAGES, LEVELS, CX, CY), f32),
            pltpu.VMEM((CX, MAIN, CY), f32),
            pltpu.VMEM((CX, CY), f32),
            pltpu.VMEM((LEVELS, 9, CX, CY), f32),
            pltpu.VMEM((STAGES, LEVELS, 2, EDGE, CY), f32),
            pltpu.VMEM((STAGES, LEVELS, 2 * CX, CY), f32),
            pltpu.VMEM((STAGES, LEVELS, 2, EDGE, CY), f32),
            pltpu.VMEM((STAGES, LEVELS, 2, 2 * CX, CY), f32),
            pltpu.VMEM((8, CY), f32),
            pltpu.VMEM((CX * LEVELS, CY), f32),
            pltpu.VMEM((4, 128, 128), f32),
            pltpu.VMEM((4, 128, 128), f32),
            pltpu.VMEM((BINS, ROWS, 128), f32),
            pltpu.VMEM((2 * ROWS, DEPTH), jnp.bfloat16),
            pltpu.VMEM((DEPTH, CAP * CY), jnp.bfloat16),
            pltpu.VMEM((CAP, ROWS, CY), f32),
            pltpu.SemaphoreType.DMA((STAGES, LEVELS, 2)),
            pltpu.SemaphoreType.DMA((STAGES, LEVELS, 2)),
            pltpu.SemaphoreType.DMA((STAGES, LEVELS, 2)),
            pltpu.SemaphoreType.DMA((STAGES, LEVELS, 2)),
            pltpu.SemaphoreType.DMA((2,)),
            pltpu.SemaphoreType.DMA((2,)),
        ],
        compiler_params=pltpu.CompilerParams(
            collective_id=0, has_side_effects=True, vmem_limit_bytes=40 * 2**20
        ),
    )(
        droplet_mass.reshape(CX * BINS * LEVELS, CY),
        wind_x.reshape(CX * LEVELS, CY),
        wind_y.reshape(CX * LEVELS, CY),
        table,
        breakup,
        target,
        fragment_low,
        cloudy,
    )
    return result.reshape(CX, BINS, LEVELS, CY)


def solution(mesh):
    in_specs = (
        P("gx", None, None, "gy"),
        P("gx", None, "gy"),
        P("gx", None, "gy"),
        P(),
        P(),
        P(),
        P(),
        P("gx", "gy"),
    )
    return jax.shard_map(
        functools.partial(local, mesh.shape["gx"], mesh.shape["gy"]),
        mesh=mesh,
        in_specs=in_specs,
        out_specs=P("gx", None, None, "gy"),
        check_vma=False,
    )
```

time: 229 us -> 52.8 us (0.23)
  the two profiles are of different devices: /device:TPU:129 before, /device:TPU:40 now
where the time goes in v1:
time: 52.8 us; the launch traced here: 52.3 us
  Pallas kernels  45.4 us (86%)
  local copies, waits for them, and re-layouts  6.92 us (13%)
    pallas_call x1, Pallas kernels, local(): pl.pallas_call(functools.partial(kernel, size_x, size_y), out_shape=jax.S...  45.4 us
    unnamed x18, local copies, waits for them, and re-layouts  6.92 us

profile of v1, /device:TPU:40, one launch (start us, length us, event | category | flops | bytes accessed | tf_op | source)
XLA Modules:
  0.0 52.3 jit_solution(11782853190565153673)
XLA Ops:
  0.0 0.0 copy-start.7
  0.0 0.7 %copy-done.7 = s32[8,1]{0,1:T(1,128)S(1)} copy-done((s32[8,1]{0,1:T(1,128)S(1)}, s32[8,1]{0,1:T(1,128)}, u32[]{:S(2)}) %copy-start.7) | copy-done | bytes 56
  0.7 0.1 copy.9.cloudy
  0.7 0.0 copy-start
  0.7 1.0 %copy-done = f32[8,33,4,128]{3,2,1,0:T(4,128)S(1)} copy-done((f32[8,33,4,128]{3,2,1,0:T(4,128)S(1)}, f32[8,33,4,128]{3,2,1,0:T(4,128)}, u32[]{:S(2)}) %copy-start) | copy-done | bytes 540696
  1.8 0.0 copy-start.1
  1.8 0.7 %copy-done.1 = f32[33,33]{1,0:T(8,128)S(1)} copy-done((f32[33,33]{1,0:T(8,128)S(1)}, f32[33,33]{1,0:T(8,128)}, u32[]{:S(2)}) %copy-start.1) | copy-done | bytes 4380
  2.5 0.0 copy-start.2
  2.5 0.7 %copy-done.2 = f32[33,33]{1,0:T(8,128)S(1)} copy-done((f32[33,33]{1,0:T(8,128)S(1)}, f32[33,33]{1,0:T(8,128)}, u32[]{:S(2)}) %copy-start.2) | copy-done | bytes 4380
  3.2 0.0 copy-start.3
  3.2 0.7 %copy-done.3 = s32[33,33]{1,0:T(8,128)S(1)} copy-done((s32[33,33]{1,0:T(8,128)S(1)}, s32[33,33]{1,0:T(8,128)}, u32[]{:S(2)}) %copy-start.3) | copy-done | bytes 4380
  4.0 0.0 copy-start.4
  4.0 0.7 %copy-done.4 = s32[33,33]{1,0:T(8,128)S(1)} copy-done((s32[33,33]{1,0:T(8,128)S(1)}, s32[33,33]{1,0:T(8,128)}, u32[]{:S(2)}) %copy-start.4) | copy-done | bytes 4380
  4.7 0.0 copy-start.5
  4.7 0.7 %copy-done.5 = f32[8,4,128]{2,1,0:T(4,128)S(1)} copy-done((f32[8,4,128]{2,1,0:T(4,128)S(1)}, f32[8,4,128]{2,1,0:T(4,128)}, u32[]{:S(2)}) %copy-start.5) | copy-done | bytes 16408
  5.4 0.0 copy-start.6
  5.4 0.7 %copy-done.6 = f32[8,4,128]{2,1,0:T(4,128)S(1)} copy-done((f32[8,4,128]{2,1,0:T(4,128)S(1)}, f32[8,4,128]{2,1,0:T(4,128)}, u32[]{:S(2)}) %copy-start.6) | copy-done | bytes 16408
  6.1 45.4 %shard_map.82 = f32[1056,128]{1,0:T(8,128)S(1)} custom-call(f32[1056,128]{1,0:T(8,128)S(1)} %bitcast.5, f32[32,128]{1,0:T(8,128)S(1)} %bitcast.6, f32[32,128]{1,0:T(8,128)S(1)} %bitcast.7, f32[33,33]{1,0:T(8,128)S(1)} %copy-done.1, f32[33,33]{1,0:T(8,128)S(1)} %copy-done.2, s32[33,33]{1,0:T(8,128)S(1)} %copy-done.3, s32[33,33]{1,0:T(8,128)S(1)} %copy-done.4, ...), custom_call_target="tpu_custom_call" | custom-call | tf_op jit(solution)/shard_map/pallas_call | solution.py:369
  51.5 0.8 %copy.11 = f32[8,33,4,128]{3,2,1,0:T(4,128)} copy(f32[8,33,4,128]{3,2,1,0:T(4,128)S(1)} %bitcast.4) | data formatting | bytes 1081344
Async XLA Ops:
  0.0 0.7 %copy-start.7 = (s32[8,1]{0,1:T(1,128)S(1)}, s32[8,1]{0,1:T(1,128)}, u32[]{:S(2)}) copy-start(s32[8,1]{0,1:T(1,128)} %param.15) | copy-start | bytes 100
  0.7 1.0 %copy-start = (f32[8,33,4,128]{3,2,1,0:T(4,128)S(1)}, f32[8,33,4,128]{3,2,1,0:T(4,128)}, u32[]{:S(2)}) copy-start(f32[8,33,4,128]{3,2,1,0:T(4,128)} %param.8) | copy-start | bytes 1622020
  1.8 0.7 %copy-start.1 = (f32[33,33]{1,0:T(8,128)S(1)}, f32[33,33]{1,0:T(8,128)}, u32[]{:S(2)}) copy-start(f32[33,33]{1,0:T(8,128)} %table_kernel.1) | copy-start | bytes 13072
  2.5 0.7 %copy-start.2 = (f32[33,33]{1,0:T(8,128)S(1)}, f32[33,33]{1,0:T(8,128)}, u32[]{:S(2)}) copy-start(f32[33,33]{1,0:T(8,128)} %table_breakup.1) | copy-start | bytes 13072
  3.2 0.7 %copy-start.3 = (s32[33,33]{1,0:T(8,128)S(1)}, s32[33,33]{1,0:T(8,128)}, u32[]{:S(2)}) copy-start(s32[33,33]{1,0:T(8,128)} %table_target.1) | copy-start | bytes 13072
  4.0 0.7 %copy-start.4 = (s32[33,33]{1,0:T(8,128)S(1)}, s32[33,33]{1,0:T(8,128)}, u32[]{:S(2)}) copy-start(s32[33,33]{1,0:T(8,128)} %table_low.1) | copy-start | bytes 13072
  4.7 0.7 %copy-start.5 = (f32[8,4,128]{2,1,0:T(4,128)S(1)}, f32[8,4,128]{2,1,0:T(4,128)}, u32[]{:S(2)}) copy-start(f32[8,4,128]{2,1,0:T(4,128)} %param.9) | copy-start | bytes 49156
  5.4 0.7 %copy-start.6 = (f32[8,4,128]{2,1,0:T(4,128)S(1)}, f32[8,4,128]{2,1,0:T(4,128)}, u32[]{:S(2)}) copy-start(f32[8,4,128]{2,1,0:T(4,128)} %param.10) | copy-start | bytes 49156

commit v2 on v1

--- a/solution.py
+++ b/solution.py
@@ -17,7 +17,9 @@
 CAP = 4
 DEPTH = 688
 ROWS = 48
-EDGE = 2 * MAIN + CX
+EDGE = 2 * MAIN + 2
+OUTER = (0, 1, CX - 2, CX - 1)
+INNER = tuple(range(2, CX - 2))
 MESH = pl.DeviceIdType.MESH
 
 
@@ -83,15 +85,21 @@
 def kernel(
     size_x,
     size_y,
-    mass,
-    wind_x,
-    wind_y,
+    mass_in,
+    wind_x_in,
+    wind_y_in,
     table_kernel,
     table_breakup,
     table_target,
     table_low,
+    cloudy_in,
+    out,
+    mass,
+    wind_x,
+    wind_y,
+    tables_f,
+    tables_i,
     cloudy,
-    out,
     state,
     last,
     moved,
@@ -103,6 +111,7 @@
     got_y,
     got_wx,
     got_wy,
+    send_wy,
     padded,
     flipped,
     parts,
@@ -115,6 +124,7 @@
     sem_ry,
     sem_sw,
     sem_rw,
+    sem_in,
 ):
     gx = lax.axis_index("gx")
     gy = lax.axis_index("gy")
@@ -131,9 +141,11 @@
             src_ref=src, dst_ref=dst, send_sem=send, recv_sem=recv, device_id=device, device_id_type=MESH
         )
 
-    def copies(stage, level):
+    def copies_x(stage, level):
         out = []
-        for side, device in ((0, west), (1, east)):
+        far = lax.rem(gx, 2)
+        for side in (far, 1 - far):
+            device = (lax.rem(gx + size_x - 1 + 2 * side, size_x), gy)
             out.append(
                 remote(
                     send_x.at[stage, level, side],
@@ -143,10 +155,14 @@
                     device,
                 )
             )
-        for side, device in ((0, south), (1, north)):
+        return out
+
+    def copies_y(stage, level):
+        out = []
+        for side, device in ((1, north), (0, south)):
             out.append(
                 remote(
-                    send_y.at[stage, level],
+                    send_y.at[stage, level, side],
                     got_y.at[stage, level, 1 - side],
                     sem_sy.at[stage, level, side],
                     sem_ry.at[stage, level, 1 - side],
@@ -155,56 +171,128 @@
             )
         return out
 
+    def copies(stage, level):
+        return copies_x(stage, level) + copies_y(stage, level)
+
     def wind_copies():
         return [
-            remote(wind_x.at[pl.ds(24, 8)], got_wx, sem_sw.at[0], sem_rw.at[0], east),
-            remote(wind_y, got_wy, sem_sw.at[1], sem_rw.at[1], north),
+            remote(wind_x_in.at[pl.ds(24, 8)], got_wx, sem_sw.at[0], sem_rw.at[0], east),
+            remote(send_wy, got_wy, sem_sw.at[1], sem_rw.at[1], north),
         ]
+
+    def packed(pack, x, value):
+        for j in range(4):
+            at = 32 * j + 4 * x
+            turned = pltpu.roll(value[8 * j : 8 * j + 8], (at - 126) % 128, 1)
+            pack = jnp.where((lane >= at) & (lane < at + 4), turned, pack)
+        return pack
+
+    def keep_row(stage, level, x, value):
+        state[stage, level, x] = value
+        if x in OUTER:
+            side, at = (0, x) if x < 2 else (1, x - (CX - 2))
+            send_x[stage, level, side, at * MAIN : (at + 1) * MAIN] = value
+
+    def keep_y(stage, level, pack, tail):
+        send_y[stage, level, 0] = jnp.where(lane < 2, tail, pack)
+        send_y[stage, level, 1] = jnp.where((lane >= 2) & (lane < 4), pltpu.roll(tail, 4, 1), pack)
 
     def keep(stage, level, values, tail):
         pack = jnp.zeros((CX, CY), jnp.float32)
-        for x in range(CX):
+        last[stage, level] = tail
+        send_x[stage, level, 0, 2 * MAIN : EDGE] = tail[0:2]
+        send_x[stage, level, 1, 2 * MAIN : EDGE] = tail[CX - 2 : CX]
+        for x in OUTER:
             value = values(x)
-            state[stage, level, x] = value
-            if x < 2:
-                send_x[stage, level, 0, x * MAIN : (x + 1) * MAIN] = value
-            if x >= CX - 2:
-                at = x - (CX - 2)
-                send_x[stage, level, 1, at * MAIN : (at + 1) * MAIN] = value
-            for j in range(4):
-                at = 32 * j + 4 * x
-                turned = pltpu.roll(value[8 * j : 8 * j + 8], (at - 126) % 128, 1)
-                pack = jnp.where((lane >= at) & (lane < at + 4), turned, pack)
-        send_x[stage, level, 0, 2 * MAIN : EDGE] = tail
-        send_x[stage, level, 1, 2 * MAIN : EDGE] = tail
-        send_y[stage, level, 0:CX] = pack
-        send_y[stage, level, CX : 2 * CX] = tail
+            keep_row(stage, level, x, value)
+            pack = packed(pack, x, value)
+        for x in INNER:
+            value = values(x)
+            keep_row(stage, level, x, value)
+            pack = packed(pack, x, value)
+        keep_y(stage, level, pack, tail)
+        for copy in copies_y(stage, level) + copies_x(stage, level):
+            copy.start()
 
     barrier = pltpu.get_barrier_semaphore()
     for device in (west, east, south, north):
         pl.semaphore_signal(barrier, inc=1, device_id=device, device_id_type=MESH)
 
-    def load(level, carry):
-        tail = mass[pl.ds(4 * MAIN + level, CX, stride=4 * BINS), :]
+    span = BINS * LEVELS
+
+    def rows_in(low, high, n):
+        rows = pl.ds(low * span, (high - low) * span)
+        return pltpu.make_async_copy(mass_in.at[rows], mass.at[rows], sem_in.at[n])
+
+    mass_copies = [rows_in(0, 2, 0), rows_in(CX - 2, CX, 1), rows_in(2, CX - 2, 2)]
+    others = [
+        pltpu.make_async_copy(src, dst, sem_in.at[3 + n])
+        for n, (src, dst) in enumerate(
+            (
+                (wind_x_in, wind_x),
+                (wind_y_in, wind_y),
+                (table_kernel, tables_f.at[0]),
+                (table_breakup, tables_f.at[1]),
+                (table_target, tables_i.at[0]),
+                (table_low, tables_i.at[1]),
+                (cloudy_in, cloudy),
+            )
+        )
+    ]
+    for copy in mass_copies + others:
+        copy.start()
+    for copy in mass_copies[:2]:
+        copy.wait()
+
+    def load_outer(level, carry):
+        for x in OUTER:
+            side, at = (0, x) if x < 2 else (1, x - (CX - 2))
+            keep_row(0, level, x, mass[pl.ds(x * span + level, MAIN, stride=4), :])
+            send_x[0, level, side, 2 * MAIN + at : 2 * MAIN + at + 1] = mass[pl.ds(x * span + 4 * MAIN + level, 1), :]
+        return carry
+
+    lax.fori_loop(0, LEVELS, load_outer, 0)
+
+    mass_copies[2].wait()
+
+    def load_inner(level, carry):
+        pack = jnp.zeros((CX, CY), jnp.float32)
+        for x in INNER:
+            keep_row(0, level, x, mass[pl.ds(x * span + level, MAIN, stride=4), :])
+        for x in range(CX):
+            pack = packed(pack, x, state[0, level, x])
+        tail = mass[pl.ds(4 * MAIN + level, CX, stride=span), :]
         last[0, level] = tail
-        keep(0, level, lambda x: mass[pl.ds(x * 4 * BINS + level, MAIN, stride=4), :], tail)
+        keep_y(0, level, pack, tail)
         return carry
 
-    lax.fori_loop(0, LEVELS, load, 0)
+    lax.fori_loop(0, LEVELS, load_inner, 0)
+    others[1].wait()
+    wind_pack = jnp.zeros((CX, CY), jnp.float32)
+    for level in range(LEVELS):
+        turned = wind_y[pl.ds(level, CX, stride=LEVELS), :]
+        wind_pack = jnp.where(lane == CY - 1 - level, pltpu.roll(turned, (CY - level) % CY, 1), wind_pack)
+    send_wy[...] = wind_pack
     pl.semaphore_wait(barrier, 4)
     for copy in wind_copies():
         copy.start()
-
-    def send_first(level, carry):
-        for copy in copies(0, level):
+    def send_first_y(level, carry):
+        for copy in copies_y(0, level):
             copy.start()
         return carry
 
+    lax.fori_loop(0, LEVELS, send_first_y, 0)
+    def send_first(level, carry):
+        for copy in copies_x(0, level):
+            copy.start()
+        return carry
+
     lax.fori_loop(0, LEVELS, send_first, 0)
-
-    build_matrix((table_kernel, table_breakup, table_target, table_low), padded, flipped, parts, matrix)
-
-    flags = [cloudy[x, 0] for x in range(CX)]
+    for copy in others[:1] + others[2:]:
+        copy.wait()
+    build_matrix((tables_f.at[0], tables_f.at[1], tables_i.at[0], tables_i.at[1]), padded, flipped, parts, matrix)
+
+    flags = [cloudy[0, x] for x in range(CX)]
     count = jnp.int32(0)
     chosen = [jnp.int32(0)] * CAP
     slots = []
@@ -222,7 +310,7 @@
         right = wind_x[pl.ds(level, CX, stride=LEVELS), :]
         left = jnp.where(row == 0, got_wx[pl.ds(4 + level, 1), :], pltpu.roll(right, 1, 0))
         above = wind_y[pl.ds(level, CX, stride=LEVELS), :]
-        ghost = got_wy[pl.ds(level, CX, stride=LEVELS), :]
+        ghost = pltpu.roll(got_wy[...], level, 1)
         below = pltpu.roll(jnp.where(lane == CY - 1, ghost, above), 1, 1)
 
         def five(low, high):
@@ -247,7 +335,7 @@
     lax.fori_loop(0, LEVELS, coefficients, 0)
 
     def advance(stage, level):
-        edge = jnp.where(lax.rem(lane, 4) < 2, got_y[stage, level, 0, 0:CX], got_y[stage, level, 1, 0:CX])
+        edge = jnp.where(lax.rem(lane, 4) < 2, got_y[stage, level, 0], got_y[stage, level, 1])
 
         def at_x(x):
             if x < 0:
@@ -273,10 +361,18 @@
 
         c = [coef[level, n] for n in range(9)]
         e = last[stage, level]
-        below_x = got_x[stage, level, 0, 2 * MAIN : EDGE]
-        above_x = got_x[stage, level, 1, 2 * MAIN : EDGE]
-        below_y = got_y[stage, level, 0, CX : 2 * CX]
-        above_y = got_y[stage, level, 1, CX : 2 * CX]
+        below_x = jnp.where(
+            row == CX - 1,
+            got_x[stage, level, 0, 2 * MAIN + 1 : 2 * MAIN + 2],
+            got_x[stage, level, 0, 2 * MAIN : 2 * MAIN + 1],
+        )
+        above_x = jnp.where(
+            row == 0,
+            got_x[stage, level, 1, 2 * MAIN : 2 * MAIN + 1],
+            got_x[stage, level, 1, 2 * MAIN + 1 : 2 * MAIN + 2],
+        )
+        below_y = pltpu.roll(got_y[stage, level, 0], CY - 4, 1)
+        above_y = got_y[stage, level, 1]
         acc = c[8] * e
         acc += c[0] * pltpu.roll(jnp.where(row >= CX - 2, below_x, e), 2, 0)
         acc += c[1] * pltpu.roll(jnp.where(row >= CX - 1, below_x, e), 1, 0)
@@ -321,7 +417,6 @@
                 copy.wait_recv()
             value, tail = advance(stage, level)
             if stage % 2 == 0:
-                last[stage + 1, level] = tail
                 keep(stage + 1, level, value, tail)
             else:
                 for x in range(CX):
@@ -338,15 +433,11 @@
                     )
                 tail = moved_last[...]
                 if stage < STAGES - 1:
-                    last[stage + 1, level] = tail
                     keep(stage + 1, level, after, tail)
                 else:
                     for x in range(CX):
                         out[pl.ds(x * 4 * BINS + level, MAIN, stride=4), :] = after(x)
                     out[pl.ds(4 * MAIN + level, CX, stride=4 * BINS), :] = tail
-            if stage < STAGES - 1:
-                for copy in copies(stage + 1, level):
-                    copy.start()
             return carry
 
         lax.fori_loop(0, LEVELS, step, 0)
@@ -369,20 +460,27 @@
     result = pl.pallas_call(
         functools.partial(kernel, size_x, size_y),
         out_shape=jax.ShapeDtypeStruct((CX * BINS * LEVELS, CY), f32),
-        in_specs=[vmem] * 7 + [pl.BlockSpec(memory_space=pltpu.SMEM)],
+        in_specs=[pl.BlockSpec(memory_space=pltpu.HBM)] * 8,
         out_specs=vmem,
         scratch_shapes=[
+            pltpu.VMEM((CX * BINS * LEVELS, CY), f32),
+            pltpu.VMEM((CX * LEVELS, CY), f32),
+            pltpu.VMEM((CX * LEVELS, CY), f32),
+            pltpu.VMEM((2, BINS, BINS), f32),
+            pltpu.VMEM((2, BINS, BINS), jnp.int32),
+            pltpu.SMEM((1, CX), jnp.int32),
             pltpu.VMEM((STAGES, LEVELS, CX, MAIN, CY), f32),
             pltpu.VMEM((STAGES, LEVELS, CX, CY), f32),
             pltpu.VMEM((CX, MAIN, CY), f32),
             pltpu.VMEM((CX, CY), f32),
             pltpu.VMEM((LEVELS, 9, CX, CY), f32),
             pltpu.VMEM((STAGES, LEVELS, 2, EDGE, CY), f32),
-            pltpu.VMEM((STAGES, LEVELS, 2 * CX, CY), f32),
+            pltpu.VMEM((STAGES, LEVELS, 2, CX, CY), f32),
             pltpu.VMEM((STAGES, LEVELS, 2, EDGE, CY), f32),
-            pltpu.VMEM((STAGES, LEVELS, 2, 2 * CX, CY), f32),
+            pltpu.VMEM((STAGES, LEVELS, 2, CX, CY), f32),
             pltpu.VMEM((8, CY), f32),
-            pltpu.VMEM((CX * LEVELS, CY), f32),
+            pltpu.VMEM((CX, CY), f32),
+            pltpu.VMEM((CX, CY), f32),
             pltpu.VMEM((4, 128, 128), f32),
             pltpu.VMEM((4, 128, 128), f32),
             pltpu.VMEM((BINS, ROWS, 128), f32),
@@ -395,9 +493,10 @@
             pltpu.SemaphoreType.DMA((STAGES, LEVELS, 2)),
             pltpu.SemaphoreType.DMA((2,)),
             pltpu.SemaphoreType.DMA((2,)),
+            pltpu.SemaphoreType.DMA((10,)),
         ],
         compiler_params=pltpu.CompilerParams(
-            collective_id=0, has_side_effects=True, vmem_limit_bytes=40 * 2**20
+            collective_id=0, has_side_effects=True, vmem_limit_bytes=62 * 2**20
         ),
     )(
         droplet_mass.reshape(CX * BINS * LEVELS, CY),
@@ -407,7 +506,7 @@
         breakup,
         target,
         fragment_low,
-        cloudy,
+        cloudy.reshape(1, CX),
     )
     return result.reshape(CX, BINS, LEVELS, CY)
 

time: 52.8 us -> 43.7 us (0.83)
  local copies, waits for them, and re-layouts: 6.92 us -> 1.88 us
  Pallas kernels: 45.4 us -> 41.7 us
    unnamed x18 -> x1, local copies, waits for them, and re-layouts: 6.92 us -> 1.88 us
    pallas_call x1, Pallas kernels: 45.4 us -> 41.7 us  [local(): pl.pallas_call(functools.partial(kernel, size_x, size_y), out_shape=jax.S...]
where the time goes in v2:
time: 43.7 us; the launch traced here: 43.6 us
  Pallas kernels  41.7 us (95%)
  local copies, waits for them, and re-layouts  1.88 us (4%)
    pallas_call x1, Pallas kernels, local(): pl.pallas_call(functools.partial(kernel, size_x, size_y), out_shape=jax.S...  41.7 us
    unnamed x1, local copies, waits for them, and re-layouts  1.88 us

profile of v2, /device:TPU:40, one launch (start us, length us, event | category | flops | bytes accessed | tf_op | source)
XLA Modules:
  0.0 43.6 jit_solution(4302908215738385390)
XLA Ops:
  0.0 41.7 %shard_map.82 = f32[1056,128]{1,0:T(8,128)} custom-call(f32[1056,128]{1,0:T(8,128)} %bitcast.6, f32[32,128]{1,0:T(8,128)} %bitcast.7, f32[32,128]{1,0:T(8,128)} %bitcast.8, f32[33,33]{1,0:T(8,128)} %table_kernel.1, f32[33,33]{1,0:T(8,128)} %table_breakup.1, s32[33,33]{1,0:T(8,128)} %table_target.1, s32[33,33]{1,0:T(8,128)} %table_low.1, s32[1,8]{1,0:T(1,128)} %bitcast.9), custom_call_target="tpu_custom_call" | custom-call | tf_op jit(solution)/shard_map/pallas_call | solution.py:460
  41.7 1.9 %copy.10 = f32[8,33,4,128]{3,2,1,0:T(4,128)} copy(f32[8,33,4,128]{3,2,1,0:T(4,128)} %bitcast.5) | data formatting | bytes 1081344

commit v3 on v2

--- a/solution.py
+++ b/solution.py
@@ -253,6 +253,15 @@
 
     lax.fori_loop(0, LEVELS, load_outer, 0)
 
+    others[1].wait()
+    wind_pack = jnp.zeros((CX, CY), jnp.float32)
+    for level in range(LEVELS):
+        turned = wind_y[pl.ds(level, CX, stride=LEVELS), :]
+        wind_pack = jnp.where(lane == CY - 1 - level, pltpu.roll(turned, (CY - level) % CY, 1), wind_pack)
+    send_wy[...] = wind_pack
+    pl.semaphore_wait(barrier, 4)
+    for copy in wind_copies():
+        copy.start()
     mass_copies[2].wait()
 
     def load_inner(level, carry):
@@ -264,30 +273,12 @@
         tail = mass[pl.ds(4 * MAIN + level, CX, stride=span), :]
         last[0, level] = tail
         keep_y(0, level, pack, tail)
-        return carry
-
-    lax.fori_loop(0, LEVELS, load_inner, 0)
-    others[1].wait()
-    wind_pack = jnp.zeros((CX, CY), jnp.float32)
-    for level in range(LEVELS):
-        turned = wind_y[pl.ds(level, CX, stride=LEVELS), :]
-        wind_pack = jnp.where(lane == CY - 1 - level, pltpu.roll(turned, (CY - level) % CY, 1), wind_pack)
-    send_wy[...] = wind_pack
-    pl.semaphore_wait(barrier, 4)
-    for copy in wind_copies():
-        copy.start()
-    def send_first_y(level, carry):
-        for copy in copies_y(0, level):
+        for copy in copies_y(0, level) + copies_x(0, level):
             copy.start()
         return carry
 
-    lax.fori_loop(0, LEVELS, send_first_y, 0)
-    def send_first(level, carry):
-        for copy in copies_x(0, level):
-            copy.start()
-        return carry
-
-    lax.fori_loop(0, LEVELS, send_first, 0)
+    lax.fori_loop(0, LEVELS, load_inner, 0)
+
     for copy in others[:1] + others[2:]:
         copy.wait()
     build_matrix((tables_f.at[0], tables_f.at[1], tables_i.at[0], tables_i.at[1]), padded, flipped, parts, matrix)
@@ -459,7 +450,7 @@
     f32 = jnp.float32
     result = pl.pallas_call(
         functools.partial(kernel, size_x, size_y),
-        out_shape=jax.ShapeDtypeStruct((CX * BINS * LEVELS, CY), f32),
+        out_shape=pltpu.VMEM((CX * BINS * LEVELS, CY), f32),
         in_specs=[pl.BlockSpec(memory_space=pltpu.HBM)] * 8,
         out_specs=vmem,
         scratch_shapes=[
@@ -496,7 +487,7 @@
             pltpu.SemaphoreType.DMA((10,)),
         ],
         compiler_params=pltpu.CompilerParams(
-            collective_id=0, has_side_effects=True, vmem_limit_bytes=62 * 2**20
+            collective_id=0, has_side_effects=True, vmem_limit_bytes=58 * 2**20
         ),
     )(
         droplet_mass.reshape(CX * BINS * LEVELS, CY),

time: 43.7 us -> 41.6 us (0.952)
  Pallas kernels: 41.7 us -> 40.6 us
  local copies, waits for them, and re-layouts: 1.88 us -> 0.8 us
    unnamed x1, local copies, waits for them, and re-layouts: 1.88 us -> 0.8 us
    pallas_call x1, Pallas kernels: 41.7 us -> 40.6 us  [local(): pl.pallas_call(functools.partial(kernel, size_x, size_y), out_shape=pltpu...]
where the time goes in v3:
time: 41.6 us; the launch traced here: 41.4 us
  Pallas kernels  40.6 us (98%)
  local copies, waits for them, and re-layouts  0.8 us (2%)
    pallas_call x1, Pallas kernels, local(): pl.pallas_call(functools.partial(kernel, size_x, size_y), out_shape=pltpu...  40.6 us

profile of v3, /device:TPU:40, one launch (start us, length us, event | category | flops | bytes accessed | tf_op | source)
XLA Modules:
  0.0 41.4 jit_solution(17544860696844655234)
XLA Ops:
  0.0 40.6 %shard_map.82 = f32[1056,128]{1,0:T(8,128)S(1)} custom-call(f32[1056,128]{1,0:T(8,128)} %bitcast.6, f32[32,128]{1,0:T(8,128)} %bitcast.7, f32[32,128]{1,0:T(8,128)} %bitcast.8, f32[33,33]{1,0:T(8,128)} %table_kernel.1, f32[33,33]{1,0:T(8,128)} %table_breakup.1, s32[33,33]{1,0:T(8,128)} %table_target.1, s32[33,33]{1,0:T(8,128)} %table_low.1, s32[1,8]{1,0:T(1,128)} %bitcast.9), custom_call_target="tpu_custom_call" | custom-call | tf_op jit(solution)/shard_map/pallas_call | solution.py:451
  40.6 0.8 %copy.10 = f32[8,33,4,128]{3,2,1,0:T(4,128)} copy(f32[8,33,4,128]{3,2,1,0:T(4,128)S(1)} %bitcast.5) | data formatting | bytes 1081344

commit v4 on v3

--- a/solution.py
+++ b/solution.py
@@ -401,11 +401,18 @@
             cols = slice(r * CY, (r + 1) * CY)
             change[r] = result[0:ROWS, cols] + result[ROWS : 2 * ROWS, cols]
 
+    for copy in wind_copies():
+        copy.wait_send()
+
     for stage in range(STAGES):
 
         def step(level, carry, stage=stage):
+            for copy in copies(stage - 1, level) if stage else []:
+                copy.wait_send()
             for copy in copies(stage, level):
                 copy.wait_recv()
+            for copy in copies(stage, level) if stage == STAGES - 1 else []:
+                copy.wait_send()
             value, tail = advance(stage, level)
             if stage % 2 == 0:
                 keep(stage + 1, level, value, tail)
@@ -432,17 +439,6 @@
             return carry
 
         lax.fori_loop(0, LEVELS, step, 0)
-
-    for copy in wind_copies():
-        copy.wait_send()
-    for stage in range(STAGES):
-
-        def finish(level, carry, stage=stage):
-            for copy in copies(stage, level):
-                copy.wait_send()
-            return carry
-
-        lax.fori_loop(0, LEVELS, finish, 0)
 
 
 def local(size_x, size_y, droplet_mass, wind_x, wind_y, table, breakup, target, fragment_low, cloudy):

time: 41.6 us -> 41.3 us (level)
  no operation moved by 1% of the time
where the time goes in v4:
time: 41.3 us; the launch traced here: 41.2 us
  Pallas kernels  40.3 us (98%)
  local copies, waits for them, and re-layouts  0.8 us (2%)
    pallas_call x1, Pallas kernels, local(): pl.pallas_call(functools.partial(kernel, size_x, size_y), out_shape=pltpu...  40.3 us

profile of v4, /device:TPU:40, one launch (start us, length us, event | category | flops | bytes accessed | tf_op | source)
XLA Modules:
  0.0 41.2 jit_solution(11298761620425016708)
XLA Ops:
  0.0 40.3 %shard_map.82 = f32[1056,128]{1,0:T(8,128)S(1)} custom-call(f32[1056,128]{1,0:T(8,128)} %bitcast.6, f32[32,128]{1,0:T(8,128)} %bitcast.7, f32[32,128]{1,0:T(8,128)} %bitcast.8, f32[33,33]{1,0:T(8,128)} %table_kernel.1, f32[33,33]{1,0:T(8,128)} %table_breakup.1, s32[33,33]{1,0:T(8,128)} %table_target.1, s32[33,33]{1,0:T(8,128)} %table_low.1, s32[1,8]{1,0:T(1,128)} %bitcast.9), custom_call_target="tpu_custom_call" | custom-call | tf_op jit(solution)/shard_map/pallas_call | solution.py:447
  40.4 0.8 %copy.10 = f32[8,33,4,128]{3,2,1,0:T(4,128)} copy(f32[8,33,4,128]{3,2,1,0:T(4,128)S(1)} %bitcast.5) | data formatting | bytes 1081344

commit v5 on v4

--- a/solution.py
+++ b/solution.py
@@ -211,7 +211,7 @@
             keep_row(stage, level, x, value)
             pack = packed(pack, x, value)
         keep_y(stage, level, pack, tail)
-        for copy in copies_y(stage, level) + copies_x(stage, level):
+        for copy in copies_x(stage, level)[:1] + copies_y(stage, level) + copies_x(stage, level)[1:]:
             copy.start()
 
     barrier = pltpu.get_barrier_semaphore()

time: 41.3 us -> 41.2 us (level)
  no operation moved by 1% of the time
where the time goes in v5:
time: 41.2 us; the launch traced here: 41.1 us
  Pallas kernels  40.3 us (98%)
  local copies, waits for them, and re-layouts  0.8 us (2%)
    pallas_call x1, Pallas kernels, local(): pl.pallas_call(functools.partial(kernel, size_x, size_y), out_shape=pltpu...  40.3 us

profile of v5, /device:TPU:40, one launch (start us, length us, event | category | flops | bytes accessed | tf_op | source)
XLA Modules:
  0.0 41.1 jit_solution(11567716223697511883)
XLA Ops:
  0.0 40.3 %shard_map.82 = f32[1056,128]{1,0:T(8,128)S(1)} custom-call(f32[1056,128]{1,0:T(8,128)} %bitcast.6, f32[32,128]{1,0:T(8,128)} %bitcast.7, f32[32,128]{1,0:T(8,128)} %bitcast.8, f32[33,33]{1,0:T(8,128)} %table_kernel.1, f32[33,33]{1,0:T(8,128)} %table_breakup.1, s32[33,33]{1,0:T(8,128)} %table_target.1, s32[33,33]{1,0:T(8,128)} %table_low.1, s32[1,8]{1,0:T(1,128)} %bitcast.9), custom_call_target="tpu_custom_call" | custom-call | tf_op jit(solution)/shard_map/pallas_call | solution.py:447
  40.3 0.8 %copy.10 = f32[8,33,4,128]{3,2,1,0:T(4,128)} copy(f32[8,33,4,128]{3,2,1,0:T(4,128)S(1)} %bitcast.5) | data formatting | bytes 1081344
